TPU v7x, 32 devices: a whole 2x2x4 slice. The times are simulated.
32 devices in a mesh: groups: 2 (over x), pool: 8 (over z, y), tp: 2 (over core).
Axes of the slice: x: 2, y: 2, z: 4, core: 2. Of those that a mesh axis runs over, the one named last changes fastest.
Arguments:
- tokens: bfloat16 [512, 8192], P('groups', 'pool'), parts along dimension 0, may hold values from -300 to 300
- gain: float32 [8192], P('pool'), may hold values from 0.1 to 1.9
- w_query: bfloat16 [8192, 8192], P('pool', 'tp'), may hold values from -0.0625 to 0.0625
- w_key: bfloat16 [8192, 1024], P('pool', 'tp'), may hold values from -0.0625 to 0.0625
- w_value: bfloat16 [8192, 1024], P('pool', 'tp'), may hold values from -0.25 to 0.25
- bias_query: float32 [8192], P('tp'), may hold values from -3 to 3
- bias_key: float32 [1024], P('tp'), may hold values from -3 to 3
- bias_value: float32 [1024], P('tp'), may hold values from -12 to 12
- w_output: bfloat16 [8192, 8192], P('tp', 'pool'), may hold values from -0.0625 to 0.0625
- cache_keys: bfloat16 [512, 160, 1024], P(('groups', 'pool'), None, 'tp'), parts along dimension 0, may hold values from -210 to 210
- cache_values: bfloat16 [512, 160, 1024], P(('groups', 'pool'), None, 'tp'), parts along dimension 0, may hold values from -24 to 24
- lengths: int32 [512], P(('groups', 'pool')), parts along dimension 0, may hold values from 1 to 160, 20480 in all
- request_of_slot: int32 [512], P('groups'), parts along dimension 0, may hold values from 0 to 255, each once
Outputs:
- attn_out: bfloat16 [512, 8192], P(('groups', 'tp'), 'pool'), parts along dimension 0
There are 2 independent parts, one for each index of `groups`. A program takes and returns all parts, laid end to end along the dimension named above; an argument that names none is the same for every part. Nothing has to cross between parts.
Inputs may be any that keep to these rules, and one draw needn't show every extreme that they name: `lengths`: the largest length is exactly 160. `request_of_slot`: a permutation of the 256 requests; slot s is held by cache owner s // 32.
All inputs are finite; a program needn't handle non-finite values. No bound on the sum of `lengths` on one device may be relied on, other than what follows from the above.
Results may differ from a plain program's by a relative error of at most 0.0075.
The roundings to bfloat16 on the way count: a program that leaves them out, or rounds other values in their place, can miss the bound.
Values may be sent and summed in bfloat16 or wider, within the bound.
A program may use at most 128 MiB of HBM per device.

v0:
```python
import jax
import jax.numpy as jnp
from jax import lax
from jax.sharding import PartitionSpec as P

D = 8192
HD = 128


ROPE_BASE = 1000000.0
EPSILON = 1e-06
NEGATIVE = -1e30


def rotate(vectors, positions):
    halfway = vectors.shape[-1] // 2
    index = jnp.arange(halfway, dtype=jnp.float32)
    freqs = ROPE_BASE ** (-2.0 * index / vectors.shape[-1])
    angles = positions.astype(jnp.float32)[:, None] * freqs[None, :]
    cosine = jnp.cos(angles)[:, None, :]
    sine = jnp.sin(angles)[:, None, :]
    former = vectors[..., :halfway]
    latter = vectors[..., halfway:]
    return jnp.concatenate(
        [former * cosine - latter * sine, latter * cosine + former * sine], axis=-1
    )


def project_rows(scaled, partial_sq, weights, pool_size):
    w_query, w_key, w_value = weights
    per_owner = partial_sq.shape[0] // pool_size
    columns = scaled.shape[1]
    chosen = scaled.reshape(pool_size, per_owner, columns).reshape(-1, columns)
    chosen_sq = partial_sq.reshape(pool_size, per_owner).reshape(-1)
    query_part = jnp.dot(chosen, w_query, preferred_element_type=jnp.float32)
    key_part = jnp.dot(chosen, w_key, preferred_element_type=jnp.float32)
    value_part = jnp.dot(chosen, w_value, preferred_element_type=jnp.float32)
    return (chosen_sq, query_part, key_part, value_part)


def attend_rows(owned, biases, caches, lengths):
    squares, query_sum, key_sum, value_sum = owned
    bias_query, bias_key, bias_value = biases
    cache_keys, cache_values = caches
    inverse = 1.0 / jnp.sqrt(squares / D + EPSILON)
    count = squares.shape[0]
    query = rotate(
        (query_sum * inverse[:, None] + bias_query).reshape(count, -1, HD), lengths
    ).astype(jnp.bfloat16)
    key_new = rotate(
        (key_sum * inverse[:, None] + bias_key).reshape(count, -1, HD), lengths
    ).astype(jnp.bfloat16)
    value_new = (
        (value_sum * inverse[:, None] + bias_value).reshape(count, -1, HD).astype(jnp.bfloat16)
    )
    kv_count = key_new.shape[1]
    span = cache_keys.shape[1]
    key_blocks = cache_keys.reshape(count, span, kv_count, HD)
    value_blocks = cache_values.reshape(count, span, kv_count, HD)
    grouped = query.reshape(count, kv_count, -1, HD)
    scaling = HD ** (-0.5)
    older = (
        jnp.einsum("nkgd,nckd->nkgc", grouped, key_blocks, preferred_element_type=jnp.float32)
        * scaling
    )
    filled = jnp.arange(span)[None, :] < lengths[:, None]
    older = jnp.where(filled[:, None, None, :], older, NEGATIVE)
    newest = (
        jnp.einsum("nkgd,nkd->nkg", grouped, key_new, preferred_element_type=jnp.float32) * scaling
    )
    highest = jnp.maximum(jnp.max(older, axis=-1), newest)
    w_old = jnp.exp(older - highest[..., None])
    w_new = jnp.exp(newest - highest)
    denominator = jnp.sum(w_old, axis=-1) + w_new
    p_old = (w_old / denominator[..., None]).astype(jnp.bfloat16)
    p_new = (w_new / denominator).astype(jnp.bfloat16)
    context = jnp.einsum("nkgc,nckd->nkgd", p_old, value_blocks, preferred_element_type=jnp.float32)
    context = (
        context
        + p_new.astype(jnp.float32)[..., None] * value_new.astype(jnp.float32)[:, :, None, :]
    )
    return context.reshape(count, -1).astype(jnp.bfloat16)


def local(
    tokens,
    gain,
    w_query,
    w_key,
    w_value,
    bias_query,
    bias_key,
    bias_value,
    w_output,
    cache_keys,
    cache_values,
    lengths,
    request_of_slot,
):
    pool_size = lax.axis_size("pool")
    total_rows = request_of_slot.shape[0]
    ordered = jnp.take(tokens, request_of_slot, axis=0)
    widened = ordered.astype(jnp.float32)
    partial_sq = jnp.sum(widened * widened, axis=1)
    scaled = (widened * gain[None, :]).astype(jnp.bfloat16)
    weights = (w_query, w_key, w_value)
    biases = (bias_query, bias_key, bias_value)
    caches = (cache_keys, cache_values)
    chosen_sq, query_part, key_part, value_part = project_rows(
        scaled, partial_sq, weights, pool_size
    )
    owned = (
        lax.psum_scatter(chosen_sq, "pool", scatter_dimension=0, tiled=True),
        lax.psum_scatter(query_part, "pool", scatter_dimension=0, tiled=True),
        lax.psum_scatter(key_part, "pool", scatter_dimension=0, tiled=True),
        lax.psum_scatter(value_part, "pool", scatter_dimension=0, tiled=True),
    )
    context = attend_rows(owned, biases, caches, lengths)
    by_slot = jnp.dot(
        lax.all_gather(context, "pool", axis=0, tiled=True),
        w_output,
        preferred_element_type=jnp.float32,
    )
    slot_of = (
        jnp.zeros((total_rows,), jnp.int32)
        .at[request_of_slot]
        .set(jnp.arange(total_rows, dtype=jnp.int32))
    )
    by_request = jnp.take(by_slot, slot_of, axis=0)
    summed = lax.psum(by_request, "tp")
    half_rows = total_rows // lax.axis_size("tp")
    result = lax.dynamic_slice_in_dim(summed, lax.axis_index("tp") * half_rows, half_rows, 0)
    return result.astype(jnp.bfloat16)


def solution(mesh):
    in_specs = (
        P("groups", "pool"),
        P("pool"),
        P("pool", "tp"),
        P("pool", "tp"),
        P("pool", "tp"),
        P("tp"),
        P("tp"),
        P("tp"),
        P("tp", "pool"),
        P(("groups", "pool"), None, "tp"),
        P(("groups", "pool"), None, "tp"),
        P(("groups", "pool")),
        P("groups"),
    )
    out_specs = P(("groups", "tp"), "pool")
    return jax.shard_map(local, mesh=mesh, in_specs=in_specs, out_specs=out_specs, check_vma=False)
```

profile of v0, /device:TPU:0, one launch (start us, length us, event | category | flops | bytes accessed | tf_op | source)
XLA Modules:
  0.0 313.8 jit_solution(11418090679363423946)
XLA Ops:
  6.5 0.8 compare_select_fusion.1
  7.4 0.7 compare_and_fusion
  8.1 2.7 gather_fusion
  10.8 2.0 fusion.25
  12.8 1.3 fusion.23
  14.3 7.8 %fusion.27 = f32[256,4096]{1,0:T(8,128)} fusion(bf16[1024,4096]{1,0:T(8,128)(2,1)} %param.15, f32[1024]{0:T(1024)S(1)} %copy-done.6, bf16[256,1024]{1,0:T(8,128)(2,1)S(1)} %gather_fusion, pred[256]{0:T(512)(128)(4,1)S(1)} %compare_and_fusion), kind=kOutput, calls=%fused_computation.30 | convolution fusion | flops 2148532224 | bytes 13111552 | tf_op jit(solution)/shard_map/dot_general | solution.py:35
  22.1 0.6 dynamic-slice
  23.7 23.1 %all-reduce = f32[256]{0:T(256)S(1)} all-reduce(f32[256]{0:T(256)S(1)} %fusion.19), channel_id=3, replica_groups=mesh['groups'=2,'pool'=8,'tp'=2] {'pool'}, use_global_device_ids=true, to_apply=%region_3.4.clone | all-reduce | flops 256 | bytes 2048
  47.1 30.5 %reduce-scatter.6.cloned.1.call-done = f32[32,512]{1,0:T(8,128)} async-done(((f32[256,512]{1,0:T(8,128)}), f32[32,512]{1,0:T(8,128)}) %reduce-scatter.6.cloned.1.call-update) | async-done | bytes 65552 | tf_op jit(solution)/shard_map/reduce_scatter | solution.py:115
  77.6 64.6 %reduce-scatter.8.cloned.1.call-done = f32[32,512]{1,0:T(8,128)} async-done(((f32[256,512]{1,0:T(8,128)}), f32[32,512]{1,0:T(8,128)}) %reduce-scatter.8.cloned.1.call-update) | async-done | bytes 65552 | tf_op jit(solution)/shard_map/reduce_scatter | solution.py:116
  142.2 1.0 fusion.33
  143.5 89.4 %reduce-scatter.4.cloned.1.call-done = f32[32,4096]{1,0:T(8,128)} async-done(((f32[256,4096]{1,0:T(8,128)}), f32[32,4096]{1,0:T(8,128)}) %reduce-scatter.4.cloned.1.call-update) | async-done | bytes 524304 | tf_op jit(solution)/shard_map/reduce_scatter | solution.py:114
  232.8 1.2 add_bitcast_fusion
  234.4 0.3 fusion.31
  234.7 5.7 %fusion.42 = (f32[32,4,8]{2,1,0:T(4,128)S(1)}, f32[32,4,8,160]{3,2,1,0:T(8,128)S(1)}) fusion(bf16[32,4,8,64]{3,2,1,0:T(8,128)(2,1)S(1)} %get-tuple-element.6, bf16[32,4,8,64]{3,2,1,0:T(8,128)(2,1)S(1)} %get-tuple-element.5, pred[32,160]{1,0:T(8,128)(4,1)S(1)} %iota_compare_fusion, bf16[32,160,512]{2,1,0:T(8,128)(2,1)} %param.22), kind=kOutput, calls=%fused_computation.65 | convolution fusion | flops 42957824 | bytes 6169600 | tf_op jit(solution)/shard_map/nkgd,nckd->nkgc/dot_general | solution.py:63
  240.5 0.5 fusion.20
  241.1 1.6 fusion.15
  242.6 0.8 copy.45
  243.5 1.6 scatter_custom_fusion
  245.1 47.6 %all-gather.2.cloned.1.call-done = bf16[256,4096]{1,0:T(8,128)(2,1)} async-done(((bf16[32,4096]{1,0:T(8,128)(2,1)}), bf16[256,4096]{1,0:T(8,128)(2,1)}) %all-gather.2.cloned.1.call-update) | async-done | bytes 2097168 | tf_op jit(solution)/shard_map/all_gather | solution.py:120
  292.7 6.3 %fusion.43 = f32[256,1024]{1,0:T(8,128)S(1)} fusion(bf16[256,4096]{1,0:T(8,128)(2,1)} %all-gather.2.cloned.1.call-done, bf16[4096,1024]{1,0:T(8,128)(2,1)} %param.21), kind=kOutput, calls=%fused_computation.66 | convolution fusion | flops 2147483648 | bytes 11534336 | tf_op jit(solution)/shard_map/dot_general | solution.py:119
  299.0 1.1 gather_fusion.1
  300.2 6.3 %all-reduce.2 = bf16[256,1024]{1,0:T(8,128)(2,1)S(1)} all-reduce(f32[256,1024]{1,0:T(8,128)S(1)} %broadcast_select_fusion), channel_id=1, replica_groups=mesh['groups'=2,'pool'=8,'tp'=2] {'tp'}, use_global_device_ids=true, to_apply=%region_8.9 | all-reduce | flops 262144 | bytes 1572864 | tf_op jit(solution)/shard_map/psum | solution.py:130
  306.5 0.7 dynamic-slice_convert_fusion
  (49 shorter events, 1.7 us)
Async XLA Ops:
  6.5 4.2 %copy-start = (bf16[1024,512]{1,0:T(8,128)(2,1)S(1)}, bf16[1024,512]{1,0:T(8,128)(2,1)}, u32[]{:S(2)}) copy-start(bf16[1024,512]{1,0:T(8,128)(2,1)} %param.16) | copy-start | bytes 3145732
  6.5 6.3 %copy-start.6 = (f32[1024]{0:T(1024)S(1)}, f32[1024]{0:T(1024)}, u32[]{:S(2)}) copy-start(f32[1024]{0:T(1024)} %param.14) | copy-start | bytes 12292
  6.5 6.3 %copy-start.5 = (bf16[1024,512]{1,0:T(8,128)(2,1)S(1)}, bf16[1024,512]{1,0:T(8,128)(2,1)}, u32[]{:S(2)}) copy-start(bf16[1024,512]{1,0:T(8,128)(2,1)} %param.17) | copy-start | bytes 3145732
  6.5 71.0 %reduce-scatter.6.cloned.1.call-start = ((), (), s32[]{:S(2)}) async-start(), calls=%async_computation.4 | async-start | bytes 589824 | tf_op jit(solution)/shard_map/reduce_scatter | solution.py:115
  12.8 129.5 %reduce-scatter.8.cloned.1.call-start = ((), (), s32[]{:S(2)}) async-start(), calls=%async_computation.5 | async-start | bytes 589824 | tf_op jit(solution)/shard_map/reduce_scatter | solution.py:116
  14.2 8.0 %copy-start.7 = (u32[32]{0:T(128)S(1)}, u32[32]{0:T(128)}, u32[]{:S(2)}) copy-start(u32[32]{0:T(128)} %constant.63) | copy-start | bytes 388
  14.2 9.2 %copy-start.4 = (s32[32]{0:T(128)S(1)}, s32[32]{0:T(128)}, u32[]{:S(2)}) copy-start(s32[32]{0:T(128)} %param.24) | copy-start | bytes 388
  14.2 128.0 %copy-start.2 = (f32[512]{0:T(512)S(1)}, f32[512]{0:T(512)}, u32[]{:S(2)}) copy-start(f32[512]{0:T(512)} %param.20) | copy-start | bytes 6148
  14.2 128.0 %copy-start.3 = (f32[512]{0:T(512)S(1)}, f32[512]{0:T(512)}, u32[]{:S(2)}) copy-start(f32[512]{0:T(512)} %param.19) | copy-start | bytes 6148
  14.2 218.6 %reduce-scatter.4.cloned.1.call-start = ((), (), s32[]{:S(2)}) async-start(), calls=%async_computation.3 | async-start | bytes 4718592 | tf_op jit(solution)/shard_map/reduce_scatter | solution.py:114
  22.0 210.8 %copy-start.1 = (f32[4096]{0:T(1024)S(1)}, f32[4096]{0:T(1024)}, u32[]{:S(2)}) copy-start(f32[4096]{0:T(1024)} %param.18) | copy-start | bytes 49156
  22.1 270.6 %all-gather.2.cloned.1.call-start = ((), (), s32[]{:S(2)}) async-start(), calls=%async_computation.6 | async-start | bytes 2359296 | tf_op jit(solution)/shard_map/all_gather | solution.py:120
  234.1 6.9 %slice-start = ((s8[5242880]{0:T(1024)(128)(4,1)}), s8[4194304]{0:T(1024)(128)(4,1)S(1)}, s32[]{:S(2)}) async-start(s8[5242880]{0:T(1024)(128)(4,1)} %bitcast.51), calls=%async_computation.7 | async-start | bytes 8388608
  234.7 6.3 %slice-start.1 = ((s8[5242880]{0:T(1024)(128)(4,1)}), s8[1048576]{0:T(1024)(128)(4,1)S(1)}, s32[]{:S(2)}) async-start(s8[5242880]{0:T(1024)(128)(4,1)} %bitcast.51), calls=%async_computation.8 | async-start | bytes 2097152
Sparse Core Ops, SparseCore 0:
  12.9 64.6 reduce-scatter.5
  81.3 60.8 reduce-scatter.7
  145.9 86.9 reduce-scatter.3
  243.6 49.0 all-gather.1
where the time goes:
time: 314 us
  waiting for transfers between devices  232 us (74%)
  blocking collectives  29.4 us (9%)
  matrix products  25 us (8%)
  between operations  14.1 us (4%)
  local copies, waits for them, and re-layouts  7.65 us (2%)
  other arithmetic  5.36 us (2%)
    reduce_scatter x1, waiting for transfers between devices, local(): lax.psum_scatter(query_part, 'pool', scatter_dimension=0, tiled=True)  89.4 us
    reduce_scatter x1, waiting for transfers between devices, local(): lax.psum_scatter(value_part, 'pool', scatter_dimension=0, tiled=True)  64.6 us
    all_gather x1, waiting for transfers between devices, local(): lax.all_gather(context, 'pool', axis=0, tiled=True)  47.6 us
    reduce_scatter x1, waiting for transfers between devices, local(): lax.psum_scatter(key_part, 'pool', scatter_dimension=0, tiled=True)  30.5 us
    unnamed x1, blocking collectives  23.1 us
    dot_general x1, matrix products, project_rows(): query_part = jnp.dot(chosen, w_query, preferred_element_type=jnp.float32)  7.78 us
    dot_general x1, matrix products, local(): jnp.dot(lax.all_gather(context, 'pool', axis=0, tiled=True), w_output, pr...  6.34 us
    psum x1, blocking collectives, local(): summed = lax.psum(by_request, 'tp')  6.29 us
  transfers between devices with their start and end apart: 4, of which 4 were waited for; matrix products, arithmetic and copies ran while one was open for 4% of the time, Pallas kernels for 0%

commit v1 on v0

v1 whole, which is shorter than its diff:
```python
import functools
import jax
import jax.numpy as jnp
from jax import lax
from jax.experimental import pallas as pl
from jax.experimental.pallas import tpu as pltpu
from jax.sharding import PartitionSpec as P

D = 8192
HD = 128


ROPE_BASE = 1000000.0
EPSILON = 1e-06
NEGATIVE = -1e30
MIB = 1 << 20
LEVELS = 32000.0


def greet(devices):
    barrier = pltpu.get_barrier_semaphore()
    for device in devices:
        pl.semaphore_signal(
            barrier, inc=1, device_id=device, device_id_type=pl.DeviceIdType.MESH
        )
    pl.semaphore_wait(barrier, len(devices))


def remote(src, dst, send, recv, device):
    return pltpu.make_async_remote_copy(
        src_ref=src,
        dst_ref=dst,
        send_sem=send,
        recv_sem=recv,
        device_id=device,
        device_id_type=pl.DeviceIdType.MESH,
    )


def lane(stats, c):
    index = lax.broadcasted_iota(jnp.int32, stats.shape, 1)
    return jnp.sum(jnp.where(index == c, stats, 0.0), axis=1, keepdims=True)


def with_lane(stats, c, column):
    index = lax.broadcasted_iota(jnp.int32, stats.shape, 1)
    return jnp.where(index == c, column, stats)


def encode(values, bound):
    factor = jnp.where(bound > 1e-30, LEVELS / jnp.maximum(bound, 1e-30), 0.0)
    return jnp.round(values * factor).astype(jnp.int32).astype(jnp.int16)


def decode(codes, bound):
    return codes.astype(jnp.int32).astype(jnp.float32) * (bound * (1.0 / LEVELS))


def layer_kernel(
    pairs,
    lengths,
    slots,
    tokens,
    gain,
    cosine,
    sine,
    bias,
    w_query,
    w_key,
    w_value,
    w_output,
    cache_keys,
    cache_values,
    out,
    weights,
    chosen,
    x,
    squares,
    mine,
    near_out,
    near_in,
    far_in,
    near_stat_out,
    near_stat_in,
    stat_sum,
    far_stat_in,
    keys,
    values,
    heads,
    key_new,
    value_new,
    out_weights,
    gathered,
    acc,
    across,
    w_sem,
    near_send,
    near_recv,
    far_send,
    far_recv,
    stat_sem,
    far_stat_send,
    far_stat_recv,
    cache_sem,
    out_w_sem,
    ctx_far_send,
    ctx_far_recv,
    ctx_near_send,
    ctx_near_recv,
    tp_sem,
):
    me = lax.axis_index("pool")
    half = lax.axis_index("tp")
    place, side = me // 2, me % 2
    chunks, depth, width = weights.shape
    query_chunks = chunks - 2
    _, _, rows, _ = mine.shape
    count = pairs * rows
    total_rows = 2 * count
    per_chunk = width // HD
    head_count = query_chunks * per_chunk
    group = head_count // per_chunk
    span = keys.shape[1]
    batches, batch = cache_sem.shape[1], rows // cache_sem.shape[1]
    partner = {"pool": place * 2 + 1 - side}
    other_core = {"tp": 1 - half}
    peers = [{"pool": lax.rem(place + d, pairs) * 2 + side} for d in range(1, pairs)]

    def query_load(c):
        columns = pl.ds(pl.multiple_of(c * width, width), width)
        return pltpu.make_async_copy(w_query.at[:, columns], weights.at[c], w_sem.at[c])

    def out_load(c):
        part = pl.ds(pl.multiple_of(c * width, width), width)
        return pltpu.make_async_copy(w_output.at[part, :], out_weights.at[c], out_w_sem.at[c])

    def cache_load(b, which):
        source, target = ((cache_keys, keys), (cache_values, values))[which]
        part = pl.ds(b * batch, batch)
        return pltpu.make_async_copy(source.at[part], target.at[part], cache_sem.at[which, b])

    def near(c):
        return remote(
            near_out.at[c], near_in.at[c], near_send.at[c], near_recv.at[c], partner
        )

    def far(c, d):
        return remote(
            near_in.at[c, lax.rem(place + d, pairs)],
            far_in.at[c, d - 1],
            far_send.at[c, d - 1],
            far_recv.at[c, d - 1],
            peers[d - 1],
        )

    def far_stat(d):
        return remote(
            stat_sum.at[lax.rem(place + d, pairs)],
            far_stat_in.at[d - 1],
            far_stat_send.at[d - 1],
            far_stat_recv.at[d - 1],
            peers[d - 1],
        )

    def ctx_far(c, d, source):
        slot = gathered.at[c, source, side]
        return remote(
            slot, slot, ctx_far_send.at[c, d - 1], ctx_far_recv.at[c, d - 1], peers[d - 1]
        )

    def ctx_near(c, which):
        slot = gathered.at[c, :, which]
        return remote(slot, slot, ctx_near_send.at[c], ctx_near_recv.at[c], partner)

    @pl.loop(0, query_chunks)
    def _(c):
        query_load(c).start()

    key_load = pltpu.make_async_copy(w_key, weights.at[chunks - 2], w_sem.at[chunks - 2])
    value_load = pltpu.make_async_copy(w_value, weights.at[chunks - 1], w_sem.at[chunks - 1])
    key_load.start()
    value_load.start()

    @pl.loop(0, batches)
    def _(b):
        cache_load(b, 0).start()
        cache_load(b, 1).start()

    @pl.loop(0, query_chunks)
    def _(c):
        out_load(c).start()

    requests = lax.broadcasted_iota(jnp.int32, (total_rows, total_rows), 0)
    chosen[...] = jnp.where(requests == slots[...], 1.0, 0.0).astype(jnp.bfloat16)
    ordered = lax.dot_general(
        chosen[...], tokens[...], (((0,), (0,)), ((), ())), preferred_element_type=jnp.float32
    )
    square = jnp.sum(ordered * ordered, axis=1, keepdims=True)
    squares[...] = jnp.broadcast_to(square, (total_rows, HD)).reshape(squares.shape)
    x[...] = (ordered * gain[...]).astype(jnp.bfloat16).reshape(x.shape)
    greet([partner, other_core] + peers)

    near_stat_out[...] = squares[:, 1 - side].reshape(count, HD)
    stat_sum[...] = squares[:, side]

    @pl.loop(0, chunks)
    def _(c):
        pltpu.make_async_copy(weights.at[c], weights.at[c], w_sem.at[c]).wait()
        part = jnp.dot(
            x[:, 1 - side].reshape(count, depth), weights[c], preferred_element_type=jnp.float32
        )
        bound = jnp.max(jnp.abs(part), axis=1, keepdims=True)
        near_stat_out[...] = with_lane(near_stat_out[...], c, bound)
        near_out[c] = encode(part, bound).reshape(pairs, rows, width)

    stat_copy = remote(near_stat_out, near_stat_in, stat_sem.at[0], stat_sem.at[1], partner)
    stat_copy.start()

    @pl.loop(0, chunks)
    def _(c):
        near(c).start()

    @pl.loop(0, chunks)
    def _(c):
        part = jnp.dot(
            x[:, side].reshape(count, depth), weights[c], preferred_element_type=jnp.float32
        )
        bound = jnp.max(jnp.abs(part), axis=1, keepdims=True)
        stat_sum[...] = with_lane(
            stat_sum[...].reshape(count, HD), c, bound
        ).reshape(stat_sum.shape)
        mine[c] = part.reshape(pairs, rows, width)

    stat_copy.wait()
    stat_sum[...] = stat_sum[...] + near_stat_in[...].reshape(stat_sum.shape)
    for d in range(1, pairs):
        far_stat(d).start()

    @pl.loop(0, chunks)
    def _(c):
        near(c).wait_recv()
        both = mine[c].reshape(count, width) + decode(
            near_in[c].reshape(count, width), lane(near_stat_in[...], c)
        )
        mine[c] = both.reshape(pairs, rows, width)
        bound = lane(stat_sum[...].reshape(count, HD), c)
        near_in[c] = encode(both, bound).reshape(pairs, rows, width)
        for d in range(1, pairs):
            far(c, d).start()

    square_sum = lane(stat_sum[place], HD - 1)
    for d in range(1, pairs):
        far_stat(d).wait_recv()
        square_sum = square_sum + lane(far_stat_in[d - 1], HD - 1)
    inverse = 1.0 / jnp.sqrt(square_sum / (depth * pairs * 2) + EPSILON)

    def finish(c):
        total = mine[c, place]
        for d in range(1, pairs):
            far(c, d).wait_recv()
            total = total + decode(far_in[c, d - 1], lane(far_stat_in[d - 1], c))
        return total * inverse + bias[pl.ds(c, 1), :]

    def turned(vectors, j):
        one = vectors[:, j * HD : (j + 1) * HD]
        return one * cosine[...] + pltpu.roll(one, HD // 2, 1) * sine[...]

    @pl.loop(0, query_chunks)
    def _(c):
        query = finish(c)
        for j in range(per_chunk):
            heads[pl.ds(c * per_chunk + j, rows, stride=head_count), :] = turned(query, j)

    key = finish(chunks - 2)
    key_new[...] = jnp.concatenate(
        [turned(key, j) for j in range(per_chunk)], axis=1
    ).astype(jnp.bfloat16).astype(jnp.float32)
    value_new[...] = finish(chunks - 1).astype(jnp.bfloat16).astype(jnp.float32)

    of_row = lax.broadcasted_iota(jnp.int32, (head_count, width), 0) // group
    of_column = lax.broadcasted_iota(jnp.int32, (head_count, width), 1) // HD
    same = of_row == of_column
    position = lax.broadcasted_iota(jnp.int32, (head_count, span), 1)
    scaling = HD ** (-0.5)

    def attend(n):
        own = pl.ds(pl.multiple_of(n * head_count, head_count), head_count)
        query = heads[own, :].astype(jnp.bfloat16).astype(jnp.float32)
        spread = jnp.where(same, jnp.concatenate([query] * per_chunk, axis=1), 0.0)
        older = lax.dot_general(
            spread.astype(jnp.bfloat16),
            keys[n],
            (((1,), (1,)), ((), ())),
            preferred_element_type=jnp.float32,
        ) * scaling
        newest = jnp.sum(spread * key_new[pl.ds(n, 1), :], axis=1, keepdims=True) * scaling
        older = jnp.where(position < lengths[n], older, NEGATIVE)
        highest = jnp.maximum(jnp.max(older, axis=1, keepdims=True), newest)
        w_old = jnp.exp(older - highest)
        w_new = jnp.exp(newest - highest)
        denominator = jnp.sum(w_old, axis=1, keepdims=True) + w_new
        p_old = (w_old / denominator).astype(jnp.bfloat16)
        p_new = (w_new / denominator).astype(jnp.bfloat16).astype(jnp.float32)
        context = jnp.dot(p_old, values[n], preferred_element_type=jnp.float32)
        context = context + p_new * value_new[pl.ds(n, 1), :]
        heads[own, :] = jnp.concatenate(
            [
                context[k * group : (k + 1) * group, k * HD : (k + 1) * HD]
                for k in range(per_chunk)
            ],
            axis=0,
        )

    @pl.loop(0, batches)
    def _(b):
        cache_load(b, 0).wait()
        cache_load(b, 1).wait()
        for j in range(batch):
            attend(b * batch + j)

    @pl.loop(0, query_chunks)
    def _(c):
        gathered[c, place, side] = jnp.concatenate(
            [
                heads[pl.ds(c * per_chunk + j, rows, stride=head_count), :]
                for j in range(per_chunk)
            ],
            axis=1,
        ).astype(jnp.bfloat16)
        for d in range(1, pairs):
            ctx_far(c, d, place).start()

    acc[...] = jnp.zeros_like(acc)

    def multiply(c):
        ctx_near(c, 1 - side).wait_recv()
        out_load(c).wait()
        by_request = jnp.dot(
            chosen[...],
            gathered[c].reshape(total_rows, width),
            preferred_element_type=jnp.float32,
        ).astype(jnp.bfloat16)
        acc[...] += jnp.dot(
            by_request, out_weights[c], preferred_element_type=jnp.float32
        ).reshape(acc.shape)

    @pl.loop(0, query_chunks)
    def _(c):
        for d in range(1, pairs):
            ctx_far(c, d, lax.rem(place + pairs - d, pairs)).wait_recv()
        ctx_near(c, side).start()

        @pl.when(c > 0)
        def _():
            multiply(c - 1)

    multiply(query_chunks - 1)
    swap = remote(acc.at[1 - half], across, tp_sem.at[0], tp_sem.at[1], other_core)
    swap.start()

    @pl.loop(0, chunks)
    def _(c):
        near(c).wait_send()
        for d in range(1, pairs):
            far(c, d).wait_send()

    @pl.loop(0, query_chunks)
    def _(c):
        ctx_near(c, side).wait_send()
        for d in range(1, pairs):
            ctx_far(c, d, place).wait_send()

    for d in range(1, pairs):
        far_stat(d).wait_send()
    swap.wait()
    out[...] = (acc[half] + across[...]).astype(jnp.bfloat16)


def local(
    tokens,
    gain,
    w_query,
    w_key,
    w_value,
    bias_query,
    bias_key,
    bias_value,
    w_output,
    cache_keys,
    cache_values,
    lengths,
    request_of_slot,
):
    pairs = lax.axis_size("pool") // 2
    total_rows, depth = tokens.shape
    count = total_rows // 2
    rows = count // pairs
    width = w_key.shape[1]
    query_chunks = w_query.shape[1] // width
    chunks = query_chunks + 2
    head_count = w_query.shape[1] // HD
    span = cache_keys.shape[1]
    columns = w_output.shape[1]
    batches = rows // 4
    index = jnp.arange(HD // 2, dtype=jnp.float32)
    freqs = ROPE_BASE ** (-2.0 * index / HD)
    angles = lengths.astype(jnp.float32)[:, None] * freqs[None, :]
    cosine, sine = jnp.cos(angles), jnp.sin(angles)
    cosine = jnp.concatenate([cosine, cosine], axis=1)
    sine = jnp.concatenate([-sine, sine], axis=1)
    bias = jnp.concatenate([bias_query, bias_key, bias_value]).reshape(chunks, width)
    vmem = pl.BlockSpec(memory_space=pltpu.VMEM)
    hbm = pl.BlockSpec(memory_space=pl.ANY)
    dma = pltpu.SemaphoreType.DMA
    bf16, f32, i16 = jnp.bfloat16, jnp.float32, jnp.int16
    return pl.pallas_call(
        functools.partial(layer_kernel, pairs),
        out_shape=jax.ShapeDtypeStruct((count, columns), bf16),
        in_specs=[pl.BlockSpec(memory_space=pltpu.SMEM)] + [vmem] * 6 + [hbm] * 6,
        out_specs=vmem,
        scratch_shapes=[
            pltpu.VMEM((chunks, depth, width), bf16),
            pltpu.VMEM((total_rows, total_rows), bf16),
            pltpu.VMEM((pairs, 2, rows, depth), bf16),
            pltpu.VMEM((pairs, 2, rows, HD), f32),
            pltpu.VMEM((chunks, pairs, rows, width), f32),
            pltpu.VMEM((chunks, pairs, rows, width), i16),
            pltpu.VMEM((chunks, pairs, rows, width), i16),
            pltpu.VMEM((chunks, pairs - 1, rows, width), i16),
            pltpu.VMEM((count, HD), f32),
            pltpu.VMEM((count, HD), f32),
            pltpu.VMEM((pairs, rows, HD), f32),
            pltpu.VMEM((pairs - 1, rows, HD), f32),
            pltpu.VMEM((rows, span, width), bf16),
            pltpu.VMEM((rows, span, width), bf16),
            pltpu.VMEM((rows * head_count, HD), f32),
            pltpu.VMEM((rows, width), f32),
            pltpu.VMEM((rows, width), f32),
            pltpu.VMEM((query_chunks, width, columns), bf16),
            pltpu.VMEM((query_chunks, pairs, 2, rows, width), bf16),
            pltpu.VMEM((2, count, columns), f32),
            pltpu.VMEM((count, columns), f32),
            dma((chunks,)),
            dma((chunks,)),
            dma((chunks,)),
            dma((chunks, pairs - 1)),
            dma((chunks, pairs - 1)),
            dma((2,)),
            dma((pairs - 1,)),
            dma((pairs - 1,)),
            dma((2, batches)),
            dma((query_chunks,)),
            dma((query_chunks, pairs - 1)),
            dma((query_chunks, pairs - 1)),
            dma((query_chunks,)),
            dma((query_chunks,)),
            dma((2,)),
        ],
        compiler_params=pltpu.CompilerParams(
            collective_id=0, has_side_effects=True, vmem_limit_bytes=62 * MIB
        ),
        cost_estimate=pl.CostEstimate(
            flops=4 * total_rows * depth * chunks * width,
            bytes_accessed=2 * depth * chunks * width + 4 * rows * span * width,
            transcendentals=rows * head_count * span,
        ),
    )(
        lengths,
        request_of_slot[None, :],
        tokens,
        gain[None, :],
        cosine,
        sine,
        bias,
        w_query,
        w_key,
        w_value,
        w_output,
        cache_keys,
        cache_values,
    )


def solution(mesh):
    in_specs = (
        P("groups", "pool"),
        P("pool"),
        P("pool", "tp"),
        P("pool", "tp"),
        P("pool", "tp"),
        P("tp"),
        P("tp"),
        P("tp"),
        P("tp", "pool"),
        P(("groups", "pool"), None, "tp"),
        P(("groups", "pool"), None, "tp"),
        P(("groups", "pool")),
        P("groups"),
    )
    out_specs = P(("groups", "tp"), "pool")
    return jax.shard_map(local, mesh=mesh, in_specs=in_specs, out_specs=out_specs, check_vma=False)
```

time: 314 us -> 102 us (0.32)
  waiting for transfers between devices: 232 us -> 0 us
  Pallas kernels: 0 us -> 96.7 us
  blocking collectives: 29.4 us -> 0 us
  matrix products: 25 us -> 0 us
  between operations: 14.1 us -> 0.02 us
  local copies, waits for them, and re-layouts: 7.65 us -> 2.29 us
    reduce_scatter x3 -> x0, waiting for transfers between devices: 184 us -> none  [the longest x1 89.4 us: local(): lax.psum_scatter(query_part, 'pool', scatter_dimension=0, tiled=True)]
    pallas_call x0 -> x1, Pallas kernels: none -> 96.7 us  [local(): pl.pallas_call(functools.partial(layer_kernel, pairs), out_shape=jax.Shap...]
    all_gather x1 -> x0, waiting for transfers between devices: 47.6 us -> none  [local(): lax.all_gather(context, 'pool', axis=0, tiled=True)]
    dot_general x7 -> x0, matrix products: 25 us -> none  [the longest x1 7.78 us: project_rows(): query_part = jnp.dot(chosen, w_query, preferred_element_type=jnp.float32)]
    unnamed x1 -> x0, blocking collectives: 23.1 us -> none
    psum x1 -> x0, blocking collectives: 6.29 us -> none  [local(): summed = lax.psum(by_request, 'tp')]
    gather x2 -> x0, local copies, waits for them, and re-layouts: 3.74 us -> none  [the longest x1 2.67 us: local(): ordered = jnp.take(tokens, request_of_slot, axis=0)]
  transfers between devices with their start and end apart: 4 -> 0, of which waited for: 4 -> 0; matrix products, arithmetic and copies ran while one was open for 4% -> 0% of each run, Pallas kernels for 0% -> 0%
where the time goes in v1:
time: 102 us; the launch traced here: 101 us
  Pallas kernels  96.7 us (95%)
  local copies, waits for them, and re-layouts  2.29 us (2%)
  other arithmetic  2.26 us (2%)
    pallas_call x1, Pallas kernels, local(): pl.pallas_call(functools.partial(layer_kernel, pairs), out_shape=jax.Shap...  96.7 us

profile of v1, /device:TPU:0, one launch (start us, length us, event | category | flops | bytes accessed | tf_op | source)
XLA Modules:
  0.0 101.3 jit_solution(15728500584914365700)
XLA Ops:
  0.0 0.7 convert_element_type.3
  0.7 0.8 pad_maximum_fusion
  1.4 0.6 reshape.9.bias
  2.0 0.1 fusion
  2.2 0.7 pad_maximum_fusion.1
  2.9 96.7 %shard_map.127 = bf16[128,1024]{1,0:T(8,128)(2,1)} custom-call(s32[32]{0:T(128)} %lengths.1, s32[1,256]{1,0:T(1,128)} %bitcast.3, bf16[256,1024]{1,0:T(8,128)(2,1)} %tokens.1, f32[1,1024]{1,0:T(1,128)} %bitcast.2, f32[32,128]{1,0:T(8,128)} %get-tuple-element.8.cosine, f32[32,128]{1,0:T(8,128)} %get-tuple-element.9.sine, f32[10,512]{1,0:T(8,128)} %reshape.9.bias, ...), custom_call_target="tpu_custom_call" | custom-call | flops 5368709120 | bytes 20971520 | tf_op jit(solution)/shard_map/pallas_call | solution.py:416
  99.6 1.7 %copy.15 = bf16[128,1024]{1,0:T(8,128)(2,1)} copy(bf16[128,1024]{1,0:T(8,128)(2,1)} %shard_map.127) | data formatting | bytes 524288
  (1 shorter events, 0.0 us)

commit v2 on v1

v2 whole, which is shorter than its diff:
```python
import functools
import math
import jax
import jax.numpy as jnp
from jax import lax
from jax.experimental import pallas as pl
from jax.experimental.pallas import tpu as pltpu
from jax.sharding import PartitionSpec as P

D = 8192
HD = 128


ROPE_BASE = 1000000.0
EPSILON = 1e-06
NEGATIVE = -1e30
MIB = 1 << 20
LEVELS = 32000.0


def greet(devices):
    barrier = pltpu.get_barrier_semaphore()
    for device in devices:
        pl.semaphore_signal(
            barrier, inc=1, device_id=device, device_id_type=pl.DeviceIdType.MESH
        )
    pl.semaphore_wait(barrier, len(devices))


def remote(src, dst, send, recv, device):
    return pltpu.make_async_remote_copy(
        src_ref=src,
        dst_ref=dst,
        send_sem=send,
        recv_sem=recv,
        device_id=device,
        device_id_type=pl.DeviceIdType.MESH,
    )


def lane(stats, c):
    index = lax.broadcasted_iota(jnp.int32, stats.shape, 1)
    return jnp.sum(jnp.where(index == c, stats, 0.0), axis=1, keepdims=True)


def with_lane(stats, c, column):
    index = lax.broadcasted_iota(jnp.int32, stats.shape, 1)
    return jnp.where(index == c, column, stats)


def encode(values, bound):
    factor = jnp.where(bound > 1e-30, LEVELS / jnp.maximum(bound, 1e-30), 0.0)
    return jnp.round(values * factor).astype(jnp.int32).astype(jnp.int16)


def decode(codes, bound):
    return codes.astype(jnp.int32).astype(jnp.float32) * (bound * (1.0 / LEVELS))


def layer_kernel(
    pairs,
    lengths,
    lengths_row,
    slots,
    tokens,
    gain,
    bias_query,
    bias_key,
    bias_value,
    w_query,
    w_key,
    w_value,
    w_output,
    cache_keys,
    cache_values,
    out,
    weights,
    chosen,
    x,
    squares,
    mine,
    near_out,
    near_in,
    far_in,
    near_stat_out,
    near_stat_in,
    stat_sum,
    far_stat_in,
    keys,
    values,
    heads,
    turns,
    key_new,
    value_new,
    out_weights,
    gathered,
    acc,
    across,
    w_sem,
    near_send,
    near_recv,
    far_send,
    far_recv,
    stat_sem,
    far_stat_send,
    far_stat_recv,
    cache_sem,
    out_w_sem,
    ctx_far_send,
    ctx_far_recv,
    ctx_near_send,
    ctx_near_recv,
    tp_sem,
):
    me = lax.axis_index("pool")
    half = lax.axis_index("tp")
    place, side = me // 2, me % 2
    chunks, depth, width = weights.shape
    query_chunks = chunks - 2
    _, _, rows, _ = mine.shape
    count = pairs * rows
    total_rows = 2 * count
    per_chunk = width // HD
    stages, per_stage, _ = heads.shape
    group = per_stage // rows
    step = query_chunks // stages
    first = 2 + step
    span = keys.shape[1]
    batch = 8
    partner = {"pool": place * 2 + 1 - side}
    other_core = {"tp": 1 - half}
    peers = [{"pool": lax.rem(place + d, pairs) * 2 + side} for d in range(1, pairs)]

    def query_load(c):
        columns = pl.ds(pl.multiple_of((c - 2) * width, width), width)
        return pltpu.make_async_copy(w_query.at[:, columns], weights.at[c], w_sem.at[c])

    def out_load(c):
        part = pl.ds(pl.multiple_of(c * width, width), width)
        return pltpu.make_async_copy(w_output.at[part, :], out_weights.at[c], out_w_sem.at[c])

    def near(c):
        return remote(
            near_out.at[c], near_in.at[c], near_send.at[c], near_recv.at[c], partner
        )

    def near_stat(g):
        return remote(
            near_stat_out.at[g], near_stat_in.at[g], stat_sem.at[0, g], stat_sem.at[1, g], partner
        )

    def far(c, d):
        return remote(
            near_in.at[c, lax.rem(place + d, pairs)],
            far_in.at[c, d - 1],
            far_send.at[c, d - 1],
            far_recv.at[c, d - 1],
            peers[d - 1],
        )

    def far_stat(g, d):
        return remote(
            stat_sum.at[g, lax.rem(place + d, pairs)],
            far_stat_in.at[g, d - 1],
            far_stat_send.at[g, d - 1],
            far_stat_recv.at[g, d - 1],
            peers[d - 1],
        )

    def ctx_far(c, d, source):
        slot = gathered.at[c, source, side]
        return remote(
            slot, slot, ctx_far_send.at[c, d - 1], ctx_far_recv.at[c, d - 1], peers[d - 1]
        )

    def ctx_near(c, which):
        slot = gathered.at[c, :, which]
        return remote(slot, slot, ctx_near_send.at[c], ctx_near_recv.at[c], partner)

    key_load = pltpu.make_async_copy(w_key, weights.at[0], w_sem.at[0])
    value_load = pltpu.make_async_copy(w_value, weights.at[1], w_sem.at[1])
    key_load.start()
    value_load.start()

    @pl.loop(2, chunks)
    def _(c):
        query_load(c).start()

    requests = lax.broadcasted_iota(jnp.int32, (total_rows, total_rows), 0)
    chosen[...] = jnp.where(requests == slots[...], 1.0, 0.0).astype(jnp.bfloat16)
    ordered = lax.dot_general(
        chosen[...], tokens[...], (((0,), (0,)), ((), ())), preferred_element_type=jnp.float32
    )
    square = jnp.sum(ordered * ordered, axis=1, keepdims=True)
    squares[...] = jnp.broadcast_to(square, (total_rows, HD)).reshape(squares.shape)
    x[...] = (ordered * gain[...]).astype(jnp.bfloat16).reshape(x.shape)
    greet([partner, other_core] + peers)

    for g, start, stop in ((0, 0, first), (1, first, chunks)):
        near_stat_out[g] = squares[:, 1 - side].reshape(count, HD)

        @pl.loop(start, stop)
        def _(c):
            pltpu.make_async_copy(weights.at[c], weights.at[c], w_sem.at[c]).wait()
            part = jnp.dot(
                x[:, 1 - side].reshape(count, depth),
                weights[c],
                preferred_element_type=jnp.float32,
            )
            bound = jnp.max(jnp.abs(part), axis=1, keepdims=True)
            near_stat_out[g] = with_lane(near_stat_out[g], c, bound)
            near_out[c] = encode(part, bound).reshape(pairs, rows, width)

        near_stat(g).start()

        @pl.loop(start, stop)
        def _(c):
            near(c).start()

    key_cache_load = pltpu.make_async_copy(cache_keys, keys, cache_sem.at[0])
    value_cache_load = pltpu.make_async_copy(cache_values, values, cache_sem.at[1])
    key_cache_load.start()
    value_cache_load.start()

    @pl.loop(0, query_chunks)
    def _(c):
        out_load(c).start()

    for g, start, stop in ((0, 0, first), (1, first, chunks)):
        stat_sum[g] = squares[:, side]

        @pl.loop(start, stop)
        def _(c):
            part = jnp.dot(
                x[:, side].reshape(count, depth), weights[c], preferred_element_type=jnp.float32
            )
            bound = jnp.max(jnp.abs(part), axis=1, keepdims=True)
            stat_sum[g] = with_lane(stat_sum[g].reshape(count, HD), c, bound).reshape(
                pairs, rows, HD
            )
            mine[c] = part.reshape(pairs, rows, width)

    def bounds(g):
        near_stat(g).wait_recv()
        stat_sum[g] = stat_sum[g] + near_stat_in[g].reshape(pairs, rows, HD)
        for d in range(1, pairs):
            far_stat(g, d).start()

    def middle(g, c):
        near(c).wait_recv()
        both = mine[c].reshape(count, width) + decode(
            near_in[c].reshape(count, width), lane(near_stat_in[g], c)
        )
        mine[c] = both.reshape(pairs, rows, width)
        bound = lane(stat_sum[g].reshape(count, HD), c)
        near_in[c] = encode(both, bound).reshape(pairs, rows, width)
        for d in range(1, pairs):
            far(c, d).start()

    bounds(0)

    @pl.loop(0, first)
    def _(c):
        middle(0, c)

    bounds(1)

    here = lax.broadcasted_iota(jnp.int32, (rows, rows), 0)
    there = lax.broadcasted_iota(jnp.int32, (rows, rows), 1)
    length = jnp.sum(
        jnp.where(here == there, lengths_row[...].astype(jnp.float32), 0.0), axis=1, keepdims=True
    )
    index = lax.broadcasted_iota(jnp.int32, (rows, HD), 1)
    index = jnp.where(index < HD // 2, index, index - HD // 2).astype(jnp.float32)
    angles = length * jnp.exp(index * (-2.0 * math.log(ROPE_BASE) / HD))
    sign = jnp.where(lax.broadcasted_iota(jnp.int32, (rows, HD), 1) < HD // 2, -1.0, 1.0)
    turns[0] = jnp.cos(angles)
    turns[1] = jnp.sin(angles) * sign

    square_sum = lane(stat_sum[0, place], HD - 1)
    for d in range(1, pairs):
        far_stat(0, d).wait_recv()
        square_sum = square_sum + lane(far_stat_in[0, d - 1], HD - 1)
    turns[2] = jnp.broadcast_to(
        1.0 / jnp.sqrt(square_sum / (depth * pairs * 2) + EPSILON), (rows, HD)
    )

    def finish(g, c, bias):
        total = mine[c, place]
        for d in range(1, pairs):
            far(c, d).wait_recv()
            total = total + decode(far_in[c, d - 1], lane(far_stat_in[g, d - 1], c))
        return total * turns[2, :, 0:1] + bias

    def turned(vectors, j):
        one = vectors[:, j * HD : (j + 1) * HD]
        return one * turns[0] + pltpu.roll(one, HD // 2, 1) * turns[1]

    key = finish(0, 0, bias_key[...])
    for j in range(stages):
        key_new[j] = turned(key, j).astype(jnp.bfloat16).astype(jnp.float32)
    value = finish(0, 1, bias_value[...])
    for j in range(stages):
        value_new[j] = value[:, j * HD : (j + 1) * HD].astype(jnp.bfloat16).astype(jnp.float32)

    position = lax.broadcasted_iota(jnp.int32, (group, span), 1)
    scaling = HD ** (-0.5)

    def repeated(ref, k, n):
        return jnp.concatenate(
            [jnp.broadcast_to(ref[k, pl.ds(n + j, 1), :], (group, HD)) for j in range(batch)],
            axis=0,
        )

    def attend(k, b):
        n = b * batch
        columns = pl.ds(pl.multiple_of(k * HD, HD), HD)
        own = pl.ds(pl.multiple_of(n * group, batch * group), batch * group)
        query = heads[k, own, :].astype(jnp.bfloat16).astype(jnp.float32)
        scores = []
        for j in range(batch):
            score = lax.dot_general(
                query[j * group : (j + 1) * group].astype(jnp.bfloat16),
                keys[n + j, :, columns],
                (((1,), (1,)), ((), ())),
                preferred_element_type=jnp.float32,
            )
            scores.append(jnp.where(position < lengths[n + j], score * scaling, NEGATIVE))
        older = jnp.concatenate(scores, axis=0)
        newest = jnp.sum(query * repeated(key_new, k, n), axis=1, keepdims=True) * scaling
        highest = jnp.maximum(jnp.max(older, axis=1, keepdims=True), newest)
        w_old = jnp.exp(older - highest)
        w_new = jnp.exp(newest - highest)
        denominator = jnp.sum(w_old, axis=1, keepdims=True) + w_new
        p_old = w_old / denominator
        p_new = (w_new / denominator).astype(jnp.bfloat16).astype(jnp.float32)
        context = jnp.concatenate(
            [
                jnp.dot(
                    p_old[j * group : (j + 1) * group].astype(jnp.bfloat16),
                    values[n + j, :, columns],
                    preferred_element_type=jnp.float32,
                )
                for j in range(batch)
            ],
            axis=0,
        )
        heads[k, own, :] = context + p_new * repeated(value_new, k, n)

    def forward(c):
        for d in range(1, pairs):
            ctx_far(c, d, lax.rem(place + pairs - d, pairs)).wait_recv()
        ctx_near(c, side).start()

    acc[...] = jnp.zeros_like(acc)

    def multiply(c):
        ctx_near(c, 1 - side).wait_recv()
        out_load(c).wait()
        by_request = jnp.dot(
            chosen[...],
            gathered[c].reshape(total_rows, width),
            preferred_element_type=jnp.float32,
        ).astype(jnp.bfloat16)
        acc[...] += jnp.dot(
            by_request, out_weights[c], preferred_element_type=jnp.float32
        ).reshape(acc.shape)

    key_cache_load.wait()
    value_cache_load.wait()

    @pl.loop(0, stages)
    def _(k):
        @pl.when(k < stages - 1)
        def _():
            @pl.loop(0, step)
            def _(i):
                middle(1, first + k * step + i)

        @pl.when(k == 1)
        def _():
            for d in range(1, pairs):
                far_stat(1, d).wait_recv()

        g = (k + stages - 2) // (stages - 1)

        @pl.loop(0, step)
        def _(i):
            c = k * step + i
            columns = pl.ds(pl.multiple_of(c * width, width), width)
            query = finish(g, 2 + c, bias_query[:, columns])
            for j in range(per_chunk):
                heads[k, pl.ds(i * per_chunk + j, rows, stride=group), :] = turned(query, j)

        @pl.loop(0, rows // batch)
        def _(b):
            attend(k, b)

        @pl.loop(0, step)
        def _(i):
            c = k * step + i
            gathered[c, place, side] = jnp.concatenate(
                [
                    heads[k, pl.ds(i * per_chunk + j, rows, stride=group), :]
                    for j in range(per_chunk)
                ],
                axis=1,
            ).astype(jnp.bfloat16)
            for d in range(1, pairs):
                ctx_far(c, d, place).start()

        @pl.when(k > 0)
        def _():
            @pl.loop(0, step)
            def _(i):
                forward((k - 1) * step + i)

    @pl.loop(0, step)
    def _(i):
        forward((stages - 1) * step + i)

    @pl.loop(0, query_chunks)
    def _(c):
        multiply(c)

    swap = remote(acc.at[1 - half], across, tp_sem.at[0], tp_sem.at[1], other_core)
    swap.start()

    @pl.loop(0, chunks)
    def _(c):
        near(c).wait_send()
        for d in range(1, pairs):
            far(c, d).wait_send()

    @pl.loop(0, query_chunks)
    def _(c):
        ctx_near(c, side).wait_send()
        for d in range(1, pairs):
            ctx_far(c, d, place).wait_send()

    for g in range(2):
        near_stat(g).wait_send()
        for d in range(1, pairs):
            far_stat(g, d).wait_send()
    swap.wait()
    out[...] = (acc[half] + across[...]).astype(jnp.bfloat16)


def local(
    tokens,
    gain,
    w_query,
    w_key,
    w_value,
    bias_query,
    bias_key,
    bias_value,
    w_output,
    cache_keys,
    cache_values,
    lengths,
    request_of_slot,
):
    pairs = lax.axis_size("pool") // 2
    total_rows, depth = tokens.shape
    count = total_rows // 2
    rows = count // pairs
    width = w_key.shape[1]
    query_chunks = w_query.shape[1] // width
    chunks = query_chunks + 2
    head_count = w_query.shape[1] // HD
    span = cache_keys.shape[1]
    columns = w_output.shape[1]
    stages = width // HD
    vmem = pl.BlockSpec(memory_space=pltpu.VMEM)
    hbm = pl.BlockSpec(memory_space=pl.ANY)
    dma = pltpu.SemaphoreType.DMA
    bf16, f32, i16 = jnp.bfloat16, jnp.float32, jnp.int16
    return pl.pallas_call(
        functools.partial(layer_kernel, pairs),
        out_shape=jax.ShapeDtypeStruct((count, columns), bf16),
        in_specs=[pl.BlockSpec(memory_space=pltpu.SMEM)] + [vmem] * 7 + [hbm] * 6,
        out_specs=vmem,
        scratch_shapes=[
            pltpu.VMEM((chunks, depth, width), bf16),
            pltpu.VMEM((total_rows, total_rows), bf16),
            pltpu.VMEM((pairs, 2, rows, depth), bf16),
            pltpu.VMEM((pairs, 2, rows, HD), f32),
            pltpu.VMEM((chunks, pairs, rows, width), f32),
            pltpu.VMEM((chunks, pairs, rows, width), i16),
            pltpu.VMEM((chunks, pairs, rows, width), i16),
            pltpu.VMEM((chunks, pairs - 1, rows, width), i16),
            pltpu.VMEM((2, count, HD), f32),
            pltpu.VMEM((2, count, HD), f32),
            pltpu.VMEM((2, pairs, rows, HD), f32),
            pltpu.VMEM((2, pairs - 1, rows, HD), f32),
            pltpu.VMEM((rows, span, width), bf16),
            pltpu.VMEM((rows, span, width), bf16),
            pltpu.VMEM((stages, rows * head_count // stages, HD), f32),
            pltpu.VMEM((3, rows, HD), f32),
            pltpu.VMEM((stages, rows, HD), f32),
            pltpu.VMEM((stages, rows, HD), f32),
            pltpu.VMEM((query_chunks, width, columns), bf16),
            pltpu.VMEM((query_chunks, pairs, 2, rows, width), bf16),
            pltpu.VMEM((2, count, columns), f32),
            pltpu.VMEM((count, columns), f32),
            dma((chunks,)),
            dma((chunks,)),
            dma((chunks,)),
            dma((chunks, pairs - 1)),
            dma((chunks, pairs - 1)),
            dma((2, 2)),
            dma((2, pairs - 1)),
            dma((2, pairs - 1)),
            dma((2,)),
            dma((query_chunks,)),
            dma((query_chunks, pairs - 1)),
            dma((query_chunks, pairs - 1)),
            dma((query_chunks,)),
            dma((query_chunks,)),
            dma((2,)),
        ],
        compiler_params=pltpu.CompilerParams(
            collective_id=0, has_side_effects=True, vmem_limit_bytes=62 * MIB
        ),
        cost_estimate=pl.CostEstimate(
            flops=4 * total_rows * depth * chunks * width,
            bytes_accessed=2 * depth * chunks * width + 4 * rows * span * width,
            transcendentals=rows * head_count * span,
        ),
    )(
        lengths,
        lengths[None, :],
        request_of_slot[None, :],
        tokens,
        gain[None, :],
        bias_query[None, :],
        bias_key[None, :],
        bias_value[None, :],
        w_query,
        w_key,
        w_value,
        w_output,
        cache_keys,
        cache_values,
    )


def solution(mesh):
    in_specs = (
        P("groups", "pool"),
        P("pool"),
        P("pool", "tp"),
        P("pool", "tp"),
        P("pool", "tp"),
        P("tp"),
        P("tp"),
        P("tp"),
        P("tp", "pool"),
        P(("groups", "pool"), None, "tp"),
        P(("groups", "pool"), None, "tp"),
        P(("groups", "pool")),
        P("groups"),
    )
    out_specs = P(("groups", "tp"), "pool")
    return jax.shard_map(local, mesh=mesh, in_specs=in_specs, out_specs=out_specs, check_vma=False)
```

time: 102 us -> 81 us (0.79)
  Pallas kernels: 96.7 us -> 79.1 us
  other arithmetic: 2.26 us -> 0 us
    pallas_call x1, Pallas kernels: 96.7 us -> 79.1 us  [local(): pl.pallas_call(functools.partial(layer_kernel, pairs), out_shape=jax.Shap...]
    concatenate x2 -> x0, other arithmetic: 1.45 us -> none  [the longest x1 0.76 us: local(): jnp.concatenate([bias_query, bias_key, bias_value]).reshape(chunks, width)]
where the time goes in v2:
time: 81 us; the launch traced here: 80.8 us
  Pallas kernels  79.1 us (98%)
  local copies, waits for them, and re-layouts  1.67 us (2%)
    pallas_call x1, Pallas kernels, local(): pl.pallas_call(functools.partial(layer_kernel, pairs), out_shape=jax.Shap...  79.1 us
    unnamed x1, local copies, waits for them, and re-layouts  1.67 us

profile of v2, /device:TPU:0, one launch (start us, length us, event | category | flops | bytes accessed | tf_op | source)
XLA Modules:
  0.0 80.8 jit_solution(15192927061455647521)
XLA Ops:
  0.0 79.1 %shard_map.127 = bf16[128,1024]{1,0:T(8,128)(2,1)} custom-call(s32[32]{0:T(128)} %lengths.1, s32[1,32]{1,0:T(1,128)} %bitcast.10, s32[1,256]{1,0:T(1,128)} %bitcast.11, bf16[256,1024]{1,0:T(8,128)(2,1)} %tokens.1, f32[1,1024]{1,0:T(1,128)} %bitcast.7, f32[1,4096]{1,0:T(1,128)} %bitcast.6, f32[1,512]{1,0:T(1,128)} %bitcast.8, f32[1,512]{1,0:T(1,128)} %bitcast.9, ...), custom_call_target="tpu_custom_call" | custom-call | flops 5368709120 | bytes 20971520 | tf_op jit(solution)/shard_map/pallas_call | solution.py:479
  79.2 1.7 %copy.15 = bf16[128,1024]{1,0:T(8,128)(2,1)} copy(bf16[128,1024]{1,0:T(8,128)(2,1)} %shard_map.127) | data formatting | bytes 524288

commit v3 on v2

--- a/solution.py
+++ b/solution.py
@@ -173,9 +173,11 @@
             slot, slot, ctx_far_send.at[c, d - 1], ctx_far_recv.at[c, d - 1], peers[d - 1]
         )
 
-    def ctx_near(c, which):
-        slot = gathered.at[c, :, which]
-        return remote(slot, slot, ctx_near_send.at[c], ctx_near_recv.at[c], partner)
+    def ctx_near(c, source, which):
+        slot = gathered.at[c, source, which]
+        return remote(
+            slot, slot, ctx_near_send.at[c, source], ctx_near_recv.at[c, source], partner
+        )
 
     key_load = pltpu.make_async_copy(w_key, weights.at[0], w_sem.at[0])
     value_load = pltpu.make_async_copy(w_value, weights.at[1], w_sem.at[1])
@@ -226,7 +228,7 @@
     def _(c):
         out_load(c).start()
 
-    for g, start, stop in ((0, 0, first), (1, first, chunks)):
+    def keep(g, start, stop):
         stat_sum[g] = squares[:, side]
 
         @pl.loop(start, stop)
@@ -257,12 +259,14 @@
         for d in range(1, pairs):
             far(c, d).start()
 
+    keep(0, 0, first)
     bounds(0)
 
     @pl.loop(0, first)
     def _(c):
         middle(0, c)
 
+    keep(1, first, chunks)
     bounds(1)
 
     here = lax.broadcasted_iota(jnp.int32, (rows, rows), 0)
@@ -349,13 +353,15 @@
 
     def forward(c):
         for d in range(1, pairs):
-            ctx_far(c, d, lax.rem(place + pairs - d, pairs)).wait_recv()
-        ctx_near(c, side).start()
+            source = lax.rem(place + pairs - d, pairs)
+            ctx_far(c, d, source).wait_recv()
+            ctx_near(c, source, side).start()
 
     acc[...] = jnp.zeros_like(acc)
 
     def multiply(c):
-        ctx_near(c, 1 - side).wait_recv()
+        for source in range(pairs):
+            ctx_near(c, source, 1 - side).wait_recv()
         out_load(c).wait()
         by_request = jnp.dot(
             chosen[...],
@@ -408,6 +414,7 @@
             ).astype(jnp.bfloat16)
             for d in range(1, pairs):
                 ctx_far(c, d, place).start()
+            ctx_near(c, place, side).start()
 
         @pl.when(k > 0)
         def _():
@@ -434,7 +441,8 @@
 
     @pl.loop(0, query_chunks)
     def _(c):
-        ctx_near(c, side).wait_send()
+        for source in range(pairs):
+            ctx_near(c, source, side).wait_send()
         for d in range(1, pairs):
             ctx_far(c, d, place).wait_send()
 
@@ -516,8 +524,8 @@
             dma((query_chunks,)),
             dma((query_chunks, pairs - 1)),
             dma((query_chunks, pairs - 1)),
-            dma((query_chunks,)),
-            dma((query_chunks,)),
+            dma((query_chunks, pairs)),
+            dma((query_chunks, pairs)),
             dma((2,)),
         ],
         compiler_params=pltpu.CompilerParams(

time: 81 us -> 79.8 us (0.985)
  Pallas kernels: 79.1 us -> 78 us
    pallas_call x1, Pallas kernels: 79.1 us -> 78 us  [local(): pl.pallas_call(functools.partial(layer_kernel, pairs), out_shape=jax.Shap...]
where the time goes in v3:
time: 79.8 us; the launch traced here: 79.7 us
  Pallas kernels  78 us (98%)
  local copies, waits for them, and re-layouts  1.67 us (2%)
    pallas_call x1, Pallas kernels, local(): pl.pallas_call(functools.partial(layer_kernel, pairs), out_shape=jax.Shap...  78 us
    unnamed x1, local copies, waits for them, and re-layouts  1.67 us

profile of v3, /device:TPU:0, one launch (start us, length us, event | category | flops | bytes accessed | tf_op | source)
XLA Modules:
  0.0 79.7 jit_solution(16924383583551610279)
XLA Ops:
  0.0 78.0 %shard_map.127 = bf16[128,1024]{1,0:T(8,128)(2,1)} custom-call(s32[32]{0:T(128)} %lengths.1, s32[1,32]{1,0:T(1,128)} %bitcast.10, s32[1,256]{1,0:T(1,128)} %bitcast.11, bf16[256,1024]{1,0:T(8,128)(2,1)} %tokens.1, f32[1,1024]{1,0:T(1,128)} %bitcast.7, f32[1,4096]{1,0:T(1,128)} %bitcast.6, f32[1,512]{1,0:T(1,128)} %bitcast.8, f32[1,512]{1,0:T(1,128)} %bitcast.9, ...), custom_call_target="tpu_custom_call" | custom-call | flops 5368709120 | bytes 20971520 | tf_op jit(solution)/shard_map/pallas_call | solution.py:487
  78.0 1.7 %copy.15 = bf16[128,1024]{1,0:T(8,128)(2,1)} copy(bf16[128,1024]{1,0:T(8,128)(2,1)} %shard_map.127) | data formatting | bytes 524288

commit v4 on v3

--- a/solution.py
+++ b/solution.py
@@ -167,10 +167,19 @@
             peers[d - 1],
         )
 
-    def ctx_far(c, d, source):
+    ways = ((0, 1), (1, -1))
+
+    def inside(at):
+        return (at >= 0) & (at < pairs)
+
+    def ctx_far(c, source, target, index):
         slot = gathered.at[c, source, side]
         return remote(
-            slot, slot, ctx_far_send.at[c, d - 1], ctx_far_recv.at[c, d - 1], peers[d - 1]
+            slot,
+            slot,
+            ctx_far_send.at[c, index],
+            ctx_far_recv.at[c, source],
+            {"pool": target * 2 + side},
         )
 
     def ctx_near(c, source, which):
@@ -352,10 +361,20 @@
         heads[k, own, :] = context + p_new * repeated(value_new, k, n)
 
     def forward(c):
-        for d in range(1, pairs):
-            source = lax.rem(place + pairs - d, pairs)
-            ctx_far(c, d, source).wait_recv()
-            ctx_near(c, source, side).start()
+        for hops in range(1, pairs):
+            for way, sign in ways:
+                source = place - sign * hops
+
+                @pl.when(inside(source))
+                def _():
+                    ctx_far(c, source, lax.rem(place + 1, pairs), 0).wait_recv()
+                    if hops > 1:
+
+                        @pl.when(inside(place + sign))
+                        def _():
+                            ctx_far(c, source, place + sign, 2 * hops + way).start()
+
+                    ctx_near(c, source, side).start()
 
     acc[...] = jnp.zeros_like(acc)
 
@@ -412,8 +431,13 @@
                 ],
                 axis=1,
             ).astype(jnp.bfloat16)
-            for d in range(1, pairs):
-                ctx_far(c, d, place).start()
+            for hops in (1, 2):
+                for way, sign in ways:
+
+                    @pl.when(inside(place + sign * hops))
+                    def _():
+                        ctx_far(c, place, place + sign * hops, 2 * hops - 2 + way).start()
+
             ctx_near(c, place, side).start()
 
         @pl.when(k > 0)
@@ -443,8 +467,20 @@
     def _(c):
         for source in range(pairs):
             ctx_near(c, source, side).wait_send()
-        for d in range(1, pairs):
-            ctx_far(c, d, place).wait_send()
+        for hops in (1, 2):
+            for way, sign in ways:
+
+                @pl.when(inside(place + sign * hops))
+                def _():
+                    ctx_far(c, place, place + sign * hops, 2 * hops - 2 + way).wait_send()
+
+        for hops in range(2, pairs):
+            for way, sign in ways:
+
+                @pl.when(inside(place - sign * hops) & inside(place + sign))
+                def _():
+                    ctx_far(c, place - sign * hops, place + sign, 2 * hops + way).wait_send()
+
 
     for g in range(2):
         near_stat(g).wait_send()
@@ -522,8 +558,8 @@
             dma((2, pairs - 1)),
             dma((2,)),
             dma((query_chunks,)),
-            dma((query_chunks, pairs - 1)),
-            dma((query_chunks, pairs - 1)),
+            dma((query_chunks, 2 * pairs)),
+            dma((query_chunks, pairs)),
             dma((query_chunks, pairs)),
             dma((query_chunks, pairs)),
             dma((2,)),

time: 79.8 us -> 78.7 us (0.986)
  Pallas kernels: 78 us -> 76.9 us
    pallas_call x1, Pallas kernels: 78 us -> 76.9 us  [local(): pl.pallas_call(functools.partial(layer_kernel, pairs), out_shape=jax.Shap...]
where the time goes in v4:
time: 78.7 us; the launch traced here: 78.6 us
  Pallas kernels  76.9 us (98%)
  local copies, waits for them, and re-layouts  1.67 us (2%)
    pallas_call x1, Pallas kernels, local(): pl.pallas_call(functools.partial(layer_kernel, pairs), out_shape=jax.Shap...  76.9 us
    unnamed x1, local copies, waits for them, and re-layouts  1.67 us

profile of v4, /device:TPU:0, one launch (start us, length us, event | category | flops | bytes accessed | tf_op | source)
XLA Modules:
  0.0 78.6 jit_solution(11329775779152287131)
XLA Ops:
  0.0 76.9 %shard_map.127 = bf16[128,1024]{1,0:T(8,128)(2,1)} custom-call(s32[32]{0:T(128)} %lengths.1, s32[1,32]{1,0:T(1,128)} %bitcast.10, s32[1,256]{1,0:T(1,128)} %bitcast.11, bf16[256,1024]{1,0:T(8,128)(2,1)} %tokens.1, f32[1,1024]{1,0:T(1,128)} %bitcast.7, f32[1,4096]{1,0:T(1,128)} %bitcast.6, f32[1,512]{1,0:T(1,128)} %bitcast.8, f32[1,512]{1,0:T(1,128)} %bitcast.9, ...), custom_call_target="tpu_custom_call" | custom-call | flops 5368709120 | bytes 20971520 | tf_op jit(solution)/shard_map/pallas_call | solution.py:523
  76.9 1.7 %copy.15 = bf16[128,1024]{1,0:T(8,128)(2,1)} copy(bf16[128,1024]{1,0:T(8,128)(2,1)} %shard_map.127) | data formatting | bytes 524288
